TPU v7x, 512 devices: a whole 4x8x8 slice. The times are simulated.
512 devices in a mesh: samp: 32 (over z, x_hi, core), par: 16 (over x_lo, y).
Axes of the slice: x: 4 (x_hi: 2, x_lo: 2; x = x_hi * 2 + x_lo), y: 8, z: 8, core: 2. Of those that a mesh axis runs over, the one named last changes fastest.
Arguments:
- activations: bfloat16 [512, 2, 64, 256], P('samp'), may hold values from 0 to 2
- cotangents: bfloat16 [512, 2, 64, 256], P('samp', None, 'par'), may hold values from -0.029907227 to 0.099609375
- energies: float32 [512], P('samp'), may hold values from -3 to -1
Outputs:
- update: float32 [64, 1152], P('par')
- coeffs: float32 [512], P('samp')
All inputs are finite; a program needn't handle non-finite values.
Results may differ from a plain program's by a relative error of at most 0.0034.
Values may be sent and summed in bfloat16 or wider, within the bound.
A program may use at most 64 MiB of HBM per device.

v0:
```python
import math
import jax
import jax.numpy as jnp
from jax import lax
from jax.sharding import PartitionSpec as P

C = 64
SIDE = 16
LAYERS = 2
reg_shift = 0.1


def sample_grads(activations, cotangents):
    sample_count, layer_count, channels, site_count = activations.shape
    owned_out = cotangents.shape[2]
    field = cotangents.reshape(sample_count, layer_count, owned_out, SIDE, SIDE)
    shifted = [
        jnp.roll(field, (row_step - 1, col_step - 1), axis=(3, 4))
        for row_step in range(3)
        for col_step in range(3)
    ]
    stacked = jnp.stack(shifted, axis=3).reshape(
        sample_count, layer_count, owned_out * 9, site_count
    )
    grads = jnp.einsum("slkx,slix->slki", stacked, activations, preferred_element_type=jnp.float32)
    grads = grads.reshape(sample_count, layer_count, owned_out, 9, channels).transpose(
        0, 2, 1, 4, 3
    )
    return grads.reshape(sample_count, owned_out * layer_count * channels * 9)


def contract(left_rows, right_rows):
    return lax.dot_general(
        left_rows, right_rows, (((1,), (1,)), ((), ())), preferred_element_type=jnp.float32
    )


def solve_system(gram, dev_all, total):
    regular = gram + reg_shift * jnp.eye(total, dtype=jnp.float32)
    factor = jnp.linalg.cholesky(regular)
    forward = lax.linalg.triangular_solve(factor, dev_all[:, None], left_side=True, lower=True)
    return lax.linalg.triangular_solve(
        factor, forward, left_side=True, lower=True, transpose_a=True
    )[:, 0]


def local(activations, cotangents, energies):
    grads = sample_grads(activations, cotangents)
    local_count = grads.shape[0]
    members = lax.axis_size("samp")
    position = lax.axis_index("samp")
    total = members * local_count
    params_all = LAYERS * C * C * 9
    scale = -math.sqrt(params_all / total)
    col_sums, energy_sum = lax.psum((jnp.sum(grads, axis=0), jnp.sum(energies)), "samp")
    centered = ((grads - col_sums / total) * (1.0 / math.sqrt(params_all))).astype(jnp.bfloat16)
    deviation = energies - energy_sum / total
    partial_value = contract(centered, lax.all_gather(centered, "samp", axis=0, tiled=True))
    summed = lax.psum(partial_value, "par")
    gram, dev_column = (
        lax.all_gather(summed, "samp", axis=0, tiled=True),
        lax.all_gather(deviation[:, None], "samp", axis=0, tiled=True),
    )
    dev_all = dev_column[:, 0]
    coeffs = solve_system(gram, dev_all, total)
    local_coeffs = lax.dynamic_slice_in_dim(coeffs, position * local_count, local_count)
    term = jnp.dot(
        local_coeffs[None, :], centered.astype(jnp.float32), precision=lax.Precision.HIGHEST
    )[0]
    summed_term = lax.psum(term, "samp")
    update = scale * summed_term
    return (update.reshape(cotangents.shape[2], -1), local_coeffs)


def solution(mesh):
    return jax.shard_map(
        local,
        mesh=mesh,
        in_specs=(P("samp", None, None, None), P("samp", None, "par", None), P("samp")),
        out_specs=(P("par", None), P("samp")),
        check_vma=False,
    )
```

profile of v0, /device:TPU:8, one launch (start us, length us, event | category | flops | bytes accessed | tf_op | source)
XLA Modules:
  0.0 767.5 jit_solution(1295712559334834222)
XLA Ops:
  7.2 1.3 reshape.131
  9.5 1.0 fusion.74
  10.5 1.2 fusion.75
  11.7 1.2 fusion.72
  12.9 1.2 fusion.73
  15.0 2.5 fusion.15
  17.5 0.9 bitcast_dynamic-update-slice_fusion.2
  18.5 1.1 fusion.16
  19.6 0.6 pad_maximum_fusion.1
  20.2 0.9 fusion.20
  21.1 0.9 copy_dynamic-update-slice_fusion
  22.0 0.9 fusion.19
  22.8 1.1 fusion.17
  24.0 0.9 bitcast_dynamic-update-slice_fusion.1
  24.8 1.1 fusion.18
  25.9 6.1 reshape.132
  32.7 2.7 copy.66
  35.7 0.6 reduce_sum.22
  36.5 76.6 %psum.30 = f32[]{:T(128)} all-reduce(f32[]{:T(128)} %reduce_sum.22), channel_id=1, replica_groups=mesh['samp'=32,'par'=16] {'samp'}, use_global_device_ids=true, to_apply=%region_12.13 | all-reduce | flops 1 | bytes 8 | tf_op jit(solution)/shard_map/psum | solution.py:55
  113.1 1.3 dynamic-slice.4
  115.8 128.5 %all-reduce.2 = (f32[4608]{0:T(1024)S(1)}, f32[512]{0:T(512)S(1)}) all-reduce(f32[4608]{0:T(1024)S(1)} %reduce_sum.21, f32[512]{0:T(512)S(1)} %subtract_dynamic-update-slice_fusion), channel_id=1, replica_groups=mesh['samp'=32,'par'=16] {'samp'}, use_global_device_ids=true, to_apply=%region_1.2 | all-reduce | flops 5120 | bytes 40960 | tf_op jit(solution)/shard_map/psum | solution.py:55
  244.3 3.4 reshape.134
  247.6 0.7 multiply_convert_fusion.1
  248.4 88.7 %all-gather.4.cloned.1.call-done = bf16[512,4608]{1,0:T(8,128)(2,1)} async-done(((bf16[16,4608]{1,0:T(8,128)(2,1)}), bf16[512,4608]{1,0:T(8,128)(2,1)}) %all-gather.4.cloned.1.call-update) | async-done | bytes 4718608 | tf_op jit(solution)/shard_map/all_gather | solution.py:58
  337.2 3.7 fusion.76
  340.9 58.7 %psum.29 = f32[16,512]{1,0:T(8,128)} all-reduce(f32[16,512]{1,0:T(8,128)S(1)} %fusion.76), channel_id=1, replica_groups=mesh['samp'=32,'par'=16] {'par'}, use_global_device_ids=true, to_apply=%region_2.3 | all-reduce | flops 8192 | bytes 65536 | tf_op jit(solution)/shard_map/psum | solution.py:59
  400.1 1.1 copy.79
  401.2 2.8 convert_element_type.12
  404.1 75.9 %all-gather.6.cloned.1.call-done = f32[512,512]{1,0:T(8,128)} async-done(((f32[16,512]{1,0:T(8,128)}), f32[512,512]{1,0:T(8,128)}) %all-gather.6.cloned.1.call-update) | async-done | bytes 1048592 | tf_op jit(solution)/shard_map/all_gather | solution.py:61
  480.0 1.6 copy.68
  481.5 1.1 select_add_fusion
  482.6 1.6 copy.69
  484.4 1.0 copy-done.1
  485.4 11.7 %cholesky.103 = f32[128,128]{1,0:T(8,128)S(1)} custom-call(f32[128,128]{1,0:T(8,128)S(1)} %cholesky.263), custom_call_target="Cholesky" | custom-call | tf_op jit(solution)/shard_map/jit(cholesky)/cholesky | solution.py:40
  497.2 9.8 %custom-call.32 = f32[1,128,128]{1,2,0:T(8,128)S(1)} custom-call(f32[1,128,128]{2,1,0:T(8,128)S(1)} %get-tuple-element.55), custom_call_target="InvertDiagBlocksLowerTriangular" | custom-call | tf_op jit(solution)/shard_map/jit(cholesky)/cholesky | solution.py:40
  507.0 1.2 fusion.25
  508.2 1.3 convolution_subtract_fusion
  509.5 11.7 %cholesky.215 = f32[128,128]{1,0:T(8,128)S(1)} custom-call(f32[128,128]{1,0:T(8,128)S(1)} %cholesky.267), custom_call_target="Cholesky" | custom-call | tf_op jit(solution)/shard_map/jit(cholesky)/cholesky | solution.py:40
  521.7 10.0 %custom-call.33 = f32[1,128,128]{1,2,0:T(8,128)S(1)} custom-call(f32[1,128,128]{2,1,0:T(8,128)S(1)} %get-tuple-element.53), custom_call_target="InvertDiagBlocksLowerTriangular" | custom-call | tf_op jit(solution)/shard_map/jit(cholesky)/cholesky | solution.py:40
  532.1 1.5 convolution_subtract_fusion.1
  533.6 11.7 %cholesky.236 = f32[128,128]{1,0:T(8,128)S(1)} custom-call(f32[128,128]{1,0:T(8,128)S(1)} %cholesky.272), custom_call_target="Cholesky" | custom-call | tf_op jit(solution)/shard_map/jit(cholesky)/cholesky | solution.py:40
  545.4 9.8 %custom-call.34 = f32[1,128,128]{1,2,0:T(8,128)S(1)} custom-call(f32[1,128,128]{2,1,0:T(8,128)S(1)} %get-tuple-element.51), custom_call_target="InvertDiagBlocksLowerTriangular" | custom-call | tf_op jit(solution)/shard_map/jit(cholesky)/cholesky | solution.py:40
  555.6 1.3 convolution_subtract_fusion.2
  556.9 12.0 %cholesky.253 = f32[128,128]{1,0:T(8,128)S(1)} custom-call(f32[128,128]{1,0:T(8,128)S(1)} %convolution_subtract_fusion.2), custom_call_target="Cholesky" | custom-call | tf_op jit(solution)/shard_map/jit(cholesky)/cholesky | solution.py:40
  569.0 0.7 compare_reduce_fusion.2
  569.7 0.6 compare_reduce_fusion.3
  570.3 0.6 compare_reduce_fusion.1
  571.0 0.7 compare_reduce_fusion
  574.3 11.3 %while.1 = (s32[]{:T(128)}, f32[512,512]{0,1:T(8,128)S(1)}, s32[4,2]{0,1:T(2,128)S(1)}, f32[4,128,128]{2,1,0:T(8,128)}, s32[]{:T(128)}) while((s32[]{:T(128)}, f32[512,512]{0,1:T(8,128)S(1)}, s32[4,2]{0,1:T(2,128)S(1)}, f32[4,128,128]{2,1,0:T(8,128)}, s32[]{:T(128)}) %tuple.39), condition=%wide.while_cond, body=%wide.while_body.sunk | while | flops 2 | bytes 393829 | solution.py:42
  574.4 0.6 fusion.100
  575.0 1.4 dynamic-slice.9
  576.5 0.6 bitcast_dynamic-update-slice_fusion.4
  577.2 0.6 fusion.100
  577.8 1.4 dynamic-slice.9
  579.4 0.6 bitcast_dynamic-update-slice_fusion.4
  580.0 0.6 fusion.100
  580.6 1.4 dynamic-slice.9
  582.2 0.6 bitcast_dynamic-update-slice_fusion.4
  582.9 0.6 fusion.100
  583.5 1.4 dynamic-slice.9
  585.0 0.6 bitcast_dynamic-update-slice_fusion.4
  585.6 40.1 %custom-call.35 = f32[4,128,128]{1,2,0:T(8,128)S(1)} custom-call(f32[4,128,128]{2,1,0:T(8,128)} %get-tuple-element.9), custom_call_target="InvertDiagBlocksLowerTriangular" | custom-call | tf_op jit(solution)/shard_map/triangular_solve | solution.py:42
  629.0 130.5 %psum.31 = f32[4608]{0:T(1024)S(1)} all-reduce(f32[4608]{0:T(1024)S(1)} %convolution_reduce_fusion), channel_id=1, replica_groups=mesh['samp'=32,'par'=16] {'samp'}, use_global_device_ids=true, to_apply=%region_13.14 | all-reduce | flops 4608 | bytes 36864 | tf_op jit(solution)/shard_map/psum | solution.py:70
  759.6 0.6 reshape.144
  (89 shorter events, 9.3 us)
Async XLA Ops:
  7.2 24.9 %copy-start = (bf16[16,2,64,256]{3,2,1,0:T(8,128)(2,1)S(1)}, bf16[16,2,64,256]{3,2,1,0:T(8,128)(2,1)}, u32[]{:S(2)}) copy-start(bf16[16,2,64,256]{3,2,1,0:T(8,128)(2,1)} %param.3) | copy-start | bytes 3145732
  7.2 330.0 %all-gather.4.cloned.1.call-start = ((), (), s32[]{:S(2)}) async-start(), calls=%async_computation | async-start | bytes 4866048 | tf_op jit(solution)/shard_map/all_gather | solution.py:58
  9.5 4.6 copy-start.7
  14.5 4.0 copy-start.2
  14.5 5.1 copy-start.3
  14.5 5.1 copy-start.4
  14.5 5.1 copy-start.5
  14.5 5.1 copy-start.6
  32.0 3.7 copy-start.9
  248.4 231.6 %all-gather.6.cloned.1.call-start = ((), (), s32[]{:S(2)}) async-start(), calls=%async_computation.1 | async-start | bytes 1081344 | tf_op jit(solution)/shard_map/all_gather | solution.py:61
  484.4 1.0 copy-start.1
  628.8 131.4 %copy-start.8 = (f32[16,1]{0,1:T(1,128)}, f32[16,1]{0,1:T(1,128)S(1)}, u32[]{:S(2)}) copy-start(f32[16,1]{0,1:T(1,128)S(1)} %fusion.59) | copy-start | bytes 196
Sparse Core Ops, SparseCore 0:
  248.5 88.6 all-gather.3
  399.8 80.1 all-gather.5
where the time goes:
time: 777 us; the launch traced here: 767 us
  blocking collectives  394 us (51%)
  waiting for transfers between devices  165 us (21%)
  other arithmetic  130 us (17%)
  local copies, waits for them, and re-layouts  46.6 us (6%)
  between operations  18.8 us (2%)
  matrix products  13.2 us (2%)
    psum x2, blocking collectives, local(): lax.psum((jnp.sum(grads, axis=0), jnp.sum(energies)), 'samp')  205 us
    psum x1, blocking collectives, local(): summed_term = lax.psum(term, 'samp')  131 us
    all_gather x1, waiting for transfers between devices, local(): lax.all_gather(centered, 'samp', axis=0, tiled=True)  88.7 us
    another operation x15, other arithmetic, solve_system(): factor = jnp.linalg.cholesky(regular)  79.5 us
    all_gather x1, waiting for transfers between devices, local(): lax.all_gather(summed, 'samp', axis=0, tiled=True)  75.9 us
    psum x1, blocking collectives, local(): summed = lax.psum(partial_value, 'par')  58.7 us
    another operation x4, other arithmetic, solve_system(): lax.linalg.triangular_solve(factor, forward, left_side=True, lower=True,...  40.4 us
  transfers between devices with their start and end apart: 2, of which 2 were waited for; matrix products, arithmetic and copies ran while one was open for 1% of the time, Pallas kernels for 0%

commit v1 on v0

--- a/solution.py
+++ b/solution.py
@@ -58,7 +58,9 @@
     partial_value = contract(centered, lax.all_gather(centered, "samp", axis=0, tiled=True))
     summed = lax.psum(partial_value, "par")
     gram, dev_column = (
-        lax.all_gather(summed, "samp", axis=0, tiled=True),
+        jnp.concatenate(
+            lax.all_to_all(jnp.stack([summed] * lax.axis_size("samp")), "samp", 0, 0), axis=0
+        ),
         lax.all_gather(deviation[:, None], "samp", axis=0, tiled=True),
     )
     dev_all = dev_column[:, 0]

time: 777 us -> 734 us (0.945)
  the two profiles are of different devices: /device:TPU:8 before, /device:TPU:2 now
where the time goes in v1:
time: 734 us; the launch traced here: 724 us
  blocking collectives  396 us (54%)
  other arithmetic  130 us (18%)
  waiting for transfers between devices  114 us (16%)
  local copies, waits for them, and re-layouts  47.8 us (7%)
  between operations  18.8 us (3%)
  matrix products  13.2 us (2%)
    psum x2, blocking collectives, local(): lax.psum((jnp.sum(grads, axis=0), jnp.sum(energies)), 'samp')  204 us
    psum x1, blocking collectives, local(): summed_term = lax.psum(term, 'samp')  128 us
    all_gather x1, waiting for transfers between devices, local(): lax.all_gather(centered, 'samp', axis=0, tiled=True)  88.9 us
    another operation x15, other arithmetic, solve_system(): factor = jnp.linalg.cholesky(regular)  79.5 us
    psum x1, blocking collectives, local(): summed = lax.psum(partial_value, 'par')  63.5 us
    another operation x4, other arithmetic, solve_system(): lax.linalg.triangular_solve(factor, forward, left_side=True, lower=True,...  40.4 us
    all_to_all x1, waiting for transfers between devices, local(): lax.all_to_all(jnp.stack([summed] * lax.axis_size('samp')), 'samp', 0, 0)  24.6 us
  transfers between devices with their start and end apart: 2, of which 2 were waited for; matrix products, arithmetic and copies ran while one was open for 1% of the time, Pallas kernels for 0%

profile of v1, /device:TPU:2, one launch (start us, length us, event | category | flops | bytes accessed | tf_op | source)
XLA Modules:
  0.0 724.0 jit_solution(5381741761960473940)
XLA Ops:
  7.2 1.3 reshape.136
  9.5 1.0 fusion.74
  10.5 1.2 fusion.75
  11.7 1.2 fusion.72
  12.9 1.2 fusion.73
  15.0 2.5 fusion.15
  17.5 0.9 bitcast_dynamic-update-slice_fusion.2
  18.5 1.1 fusion.16
  20.2 0.9 fusion.20
  21.1 0.9 copy_dynamic-update-slice_fusion
  22.0 0.9 fusion.19
  22.8 1.1 fusion.17
  24.0 0.9 bitcast_dynamic-update-slice_fusion.1
  24.8 1.1 fusion.18
  25.9 6.1 reshape.137
  32.7 2.7 copy.66
  35.7 0.6 reduce_sum.22
  36.5 75.7 %psum.30 = f32[]{:T(128)} all-reduce(f32[]{:T(128)} %reduce_sum.22), channel_id=1, replica_groups=mesh['samp'=32,'par'=16] {'samp'}, use_global_device_ids=true, to_apply=%region_12.13 | all-reduce | flops 1 | bytes 8 | tf_op jit(solution)/shard_map/psum | solution.py:55
  112.2 1.3 dynamic-slice.4
  114.9 128.5 %all-reduce.2 = (f32[4608]{0:T(1024)S(1)}, f32[512]{0:T(512)S(1)}) all-reduce(f32[4608]{0:T(1024)S(1)} %reduce_sum.21, f32[512]{0:T(512)S(1)} %subtract_dynamic-update-slice_fusion), channel_id=1, replica_groups=mesh['samp'=32,'par'=16] {'samp'}, use_global_device_ids=true, to_apply=%region_1.2 | all-reduce | flops 5120 | bytes 40960 | tf_op jit(solution)/shard_map/psum | solution.py:55
  243.4 3.4 reshape.139
  246.7 0.7 multiply_convert_fusion.1
  247.5 88.9 %all-gather.3.cloned.1.call-done = bf16[512,4608]{1,0:T(8,128)(2,1)} async-done(((bf16[16,4608]{1,0:T(8,128)(2,1)}), bf16[512,4608]{1,0:T(8,128)(2,1)}) %all-gather.3.cloned.1.call-update) | async-done | bytes 4718608 | tf_op jit(solution)/shard_map/all_gather | solution.py:58
  336.3 3.7 fusion.76
  340.1 63.5 %psum.29 = f32[16,512]{1,0:T(8,128)S(1)} all-reduce(f32[16,512]{1,0:T(8,128)S(1)} %fusion.76), channel_id=1, replica_groups=mesh['samp'=32,'par'=16] {'par'}, use_global_device_ids=true, to_apply=%region_2.3 | all-reduce | flops 8192 | bytes 65536 | tf_op jit(solution)/shard_map/psum | solution.py:59
  403.6 1.2 stack.32
  404.7 4.7 all-to-all-start
  409.9 1.1 copy.79
  411.0 2.8 convert_element_type.12
  413.8 24.6 %all-to-all-done = f32[32,16,512]{2,1,0:T(8,128)} async-done(((f32[32,16,512]{2,1,0:T(8,128)}), f32[32,16,512]{2,1,0:T(8,128)}, u32[]{:S(2)}, u32[]{:S(2)}) %all-to-all-start) | async-done | bytes 1048608 | tf_op jit(solution)/shard_map/all_to_all | solution.py:62
  438.5 1.6 copy.68
  440.0 1.1 select_add_fusion
  441.1 1.6 copy.69
  442.9 1.0 copy-done.1
  443.9 11.7 %cholesky.103 = f32[128,128]{1,0:T(8,128)S(1)} custom-call(f32[128,128]{1,0:T(8,128)S(1)} %cholesky.263), custom_call_target="Cholesky" | custom-call | tf_op jit(solution)/shard_map/jit(cholesky)/cholesky | solution.py:40
  455.7 9.8 %custom-call.32 = f32[1,128,128]{1,2,0:T(8,128)S(1)} custom-call(f32[1,128,128]{2,1,0:T(8,128)S(1)} %get-tuple-element.55), custom_call_target="InvertDiagBlocksLowerTriangular" | custom-call | tf_op jit(solution)/shard_map/jit(cholesky)/cholesky | solution.py:40
  465.5 1.2 fusion.25
  466.7 1.3 convolution_subtract_fusion
  468.0 11.7 %cholesky.215 = f32[128,128]{1,0:T(8,128)S(1)} custom-call(f32[128,128]{1,0:T(8,128)S(1)} %cholesky.267), custom_call_target="Cholesky" | custom-call | tf_op jit(solution)/shard_map/jit(cholesky)/cholesky | solution.py:40
  480.2 10.0 %custom-call.33 = f32[1,128,128]{1,2,0:T(8,128)S(1)} custom-call(f32[1,128,128]{2,1,0:T(8,128)S(1)} %get-tuple-element.53), custom_call_target="InvertDiagBlocksLowerTriangular" | custom-call | tf_op jit(solution)/shard_map/jit(cholesky)/cholesky | solution.py:40
  490.6 1.5 convolution_subtract_fusion.1
  492.1 11.7 %cholesky.236 = f32[128,128]{1,0:T(8,128)S(1)} custom-call(f32[128,128]{1,0:T(8,128)S(1)} %cholesky.272), custom_call_target="Cholesky" | custom-call | tf_op jit(solution)/shard_map/jit(cholesky)/cholesky | solution.py:40
  504.0 9.8 %custom-call.34 = f32[1,128,128]{1,2,0:T(8,128)S(1)} custom-call(f32[1,128,128]{2,1,0:T(8,128)S(1)} %get-tuple-element.51), custom_call_target="InvertDiagBlocksLowerTriangular" | custom-call | tf_op jit(solution)/shard_map/jit(cholesky)/cholesky | solution.py:40
  514.1 1.3 convolution_subtract_fusion.2
  515.4 11.9 %cholesky.253 = f32[128,128]{1,0:T(8,128)S(1)} custom-call(f32[128,128]{1,0:T(8,128)S(1)} %convolution_subtract_fusion.2), custom_call_target="Cholesky" | custom-call | tf_op jit(solution)/shard_map/jit(cholesky)/cholesky | solution.py:40
  527.5 0.7 compare_reduce_fusion.2
  528.2 0.6 compare_reduce_fusion.3
  528.9 0.6 compare_reduce_fusion.1
  529.5 0.7 compare_reduce_fusion
  532.8 11.3 %while.1 = (s32[]{:T(128)}, f32[512,512]{0,1:T(8,128)S(1)}, s32[4,2]{0,1:T(2,128)S(1)}, f32[4,128,128]{2,1,0:T(8,128)}, s32[]{:T(128)}) while((s32[]{:T(128)}, f32[512,512]{0,1:T(8,128)S(1)}, s32[4,2]{0,1:T(2,128)S(1)}, f32[4,128,128]{2,1,0:T(8,128)}, s32[]{:T(128)}) %tuple.39), condition=%wide.while_cond, body=%wide.while_body.sunk | while | flops 2 | bytes 393829 | solution.py:42
  532.9 0.6 fusion.100
  533.5 1.4 dynamic-slice.9
  535.0 0.6 bitcast_dynamic-update-slice_fusion.4
  535.7 0.6 fusion.100
  536.3 1.4 dynamic-slice.9
  537.9 0.6 bitcast_dynamic-update-slice_fusion.4
  539.2 1.4 dynamic-slice.9
  540.7 0.6 bitcast_dynamic-update-slice_fusion.4
  541.4 0.6 fusion.100
  542.0 1.4 dynamic-slice.9
  543.5 0.6 bitcast_dynamic-update-slice_fusion.4
  544.1 40.1 %custom-call.35 = f32[4,128,128]{1,2,0:T(8,128)S(1)} custom-call(f32[4,128,128]{2,1,0:T(8,128)} %get-tuple-element.9), custom_call_target="InvertDiagBlocksLowerTriangular" | custom-call | tf_op jit(solution)/shard_map/triangular_solve | solution.py:42
  587.6 128.5 %psum.31 = f32[4608]{0:T(1024)S(1)} all-reduce(f32[4608]{0:T(1024)S(1)} %convolution_reduce_fusion), channel_id=1, replica_groups=mesh['samp'=32,'par'=16] {'samp'}, use_global_device_ids=true, to_apply=%region_13.14 | all-reduce | flops 4608 | bytes 36864 | tf_op jit(solution)/shard_map/psum | solution.py:72
  716.0 0.6 reshape.150
  (89 shorter events, 10.4 us)
Async XLA Ops:
  7.2 24.9 %copy-start = (bf16[16,2,64,256]{3,2,1,0:T(8,128)(2,1)S(1)}, bf16[16,2,64,256]{3,2,1,0:T(8,128)(2,1)}, u32[]{:S(2)}) copy-start(bf16[16,2,64,256]{3,2,1,0:T(8,128)(2,1)} %param.3) | copy-start | bytes 3145732
  7.2 329.1 %all-gather.3.cloned.1.call-start = ((), (), s32[]{:S(2)}) async-start(), calls=%async_computation.1 | async-start | bytes 4866048 | tf_op jit(solution)/shard_map/all_gather | solution.py:58
  9.5 4.6 copy-start.7
  14.5 4.0 copy-start.2
  14.5 5.1 copy-start.3
  14.5 5.1 copy-start.4
  14.5 5.1 copy-start.5
  14.5 5.1 copy-start.6
  32.0 3.7 copy-start.9
  404.7 33.8 %all-to-all-start = ((f32[32,16,512]{2,1,0:T(8,128)}), f32[32,16,512]{2,1,0:T(8,128)}, u32[]{:S(2)}, u32[]{:S(2)}) async-start(f32[32,16,512]{2,1,0:T(8,128)} %stack.32), calls=%async_computation | async-start | bytes 2097152 | tf_op jit(solution)/shard_map/all_to_all | solution.py:62
  442.9 1.0 copy-start.1
  587.3 129.4 %copy-start.8 = (f32[16,1]{0,1:T(1,128)}, f32[16,1]{0,1:T(1,128)S(1)}, u32[]{:S(2)}) copy-start(f32[16,1]{0,1:T(1,128)S(1)} %fusion.59) | copy-start | bytes 196
Sparse Core Ops, SparseCore 0:
  247.6 88.6 all-gather.2
